TPU v7x, 32 devices: a whole 2x2x4 slice. The times are simulated.
32 devices in a mesh: groups: 2 (over y), row: 4 (over x, core), col: 4 (over z).
Axes of the slice: x: 2, y: 2, z: 4, core: 2. Of those that a mesh axis runs over, the one named last changes fastest.
Arguments:
- pair: bfloat16 [128, 64, 128], P(('groups', 'row'), 'col'), parts along dimension 0, may hold values from -6 to 6
- res_mask: int32 [128], P('groups'), parts along dimension 0, may hold values 0 or 1
- input_norm_gain: float32 [128], replicated, may hold values from 0.25 to 1.75
- input_norm_bias: float32 [128], replicated, may hold values from -3 to 3
- proj_left: bfloat16 [128, 256], replicated, may hold values from -0.5 to 0.5
- proj_right: bfloat16 [128, 256], replicated, may hold values from -0.5 to 0.5
- gate_out: bfloat16 [128, 128], replicated, may hold values from -0.5 to 0.5
- mid_gain: float32 [128], replicated, may hold values from 0.25 to 1.75
- mid_bias: float32 [128], replicated, may hold values from -3 to 3
- proj_out: bfloat16 [128, 128], replicated, may hold values from -0.5 to 0.5
- cotangent: bfloat16 [128, 64, 128], P(('groups', 'row'), 'col'), parts along dimension 0, may hold values from -6 to 6
Outputs:
- update: bfloat16 [128, 64, 128], P(('groups', 'row'), 'col'), parts along dimension 0
- pair_gradient: float32 [128, 64, 128], P(('groups', 'row'), 'col'), parts along dimension 0
- gain_gradient: float32 [256], P('groups'), parts along dimension 0
- grad_bias: float32 [256], P('groups'), parts along dimension 0
There are 2 independent parts, one for each index of `groups`. A program takes and returns all parts, laid end to end along the dimension named above; an argument that names none is the same for every part. Nothing has to cross between parts.
Inputs may be any that keep to these rules, and one draw needn't show every extreme that they name: `res_mask`: 1 marks a present residue, 0 a padded one.
All inputs are finite; a program needn't handle non-finite values.
Results may differ from a plain program's by a relative error of at most 0.0074.
Values may be sent and summed in bfloat16 or wider, within the bound.
A program may use at most 64 MiB of HBM per device.

v0:
```python
import jax
import jax.numpy as jnp
from jax import lax
from jax.sharding import PartitionSpec as P


def broadcast(array, axis, root):
    mine = lax.axis_index(axis) == root
    return lax.psum(jnp.where(mine, array, jnp.zeros_like(array)), axis)


def from_behind(value, axis, steps):
    count = lax.axis_size(axis)
    pairs = [(source, (source + steps) % count) for source in range(count)]
    return lax.ppermute(value, axis, pairs)


def apply_layer_norm(values):
    center = values - jnp.mean(values, axis=-1, keepdims=True)
    reciprocal_deviation = lax.rsqrt(jnp.mean(center * center, axis=-1, keepdims=True) + 1e-05)
    return (center * reciprocal_deviation, reciprocal_deviation)


def layer_norm_backward(grad_hat, hatted, reciprocal_deviation):
    first = jnp.mean(grad_hat, axis=-1, keepdims=True)
    second = jnp.mean(grad_hat * hatted, axis=-1, keepdims=True)
    return (grad_hat - first - hatted * second) * reciprocal_deviation


def gating_back(grad_out, raw, pmask, width):
    sig = jax.nn.sigmoid(raw[..., :width])
    val = raw[..., width:]
    masked = grad_out * pmask
    return jnp.concatenate([masked * val * sig * (1.0 - sig), masked * sig], axis=-1).astype(
        jnp.bfloat16
    )


def outer_add(running, left_block, right_block):
    return running + jnp.einsum(
        "ikc,jkc->ijc", left_block, right_block, preferred_element_type=jnp.float32
    )


def on_device(
    pair,
    res_mask,
    input_norm_gain,
    input_norm_bias,
    proj_left,
    proj_right,
    gate_out,
    mid_gain,
    mid_bias,
    proj_out,
    cotangent,
):
    rows, cols, chans = pair.shape
    hidden = proj_left.shape[1] // 2
    total_res = res_mask.shape[0]
    width = lax.axis_size("col")
    row_index = lax.axis_index("row")
    col_index = lax.axis_index("col")
    maskf = res_mask.astype(jnp.float32)
    mask_rows = lax.dynamic_slice_in_dim(maskf, row_index * rows, rows)
    mask_cols = lax.dynamic_slice_in_dim(maskf, col_index * cols, cols)
    pmask = (mask_rows[:, None] * mask_cols[None, :])[..., None]
    standardized_input, reciprocal_deviation = apply_layer_norm(pair.astype(jnp.float32))
    normalized_pair = (standardized_input * input_norm_gain + input_norm_bias).astype(jnp.bfloat16)
    flat = normalized_pair.reshape(rows * cols, chans)
    left = jnp.dot(flat, proj_left, preferred_element_type=jnp.float32).reshape(
        rows, cols, 2 * hidden
    )
    right = jnp.dot(flat, proj_right, preferred_element_type=jnp.float32).reshape(
        rows, cols, 2 * hidden
    )
    left_gated = (pmask * jax.nn.sigmoid(left[..., :hidden]) * left[..., hidden:]).astype(
        jnp.bfloat16
    )
    right_gated = (pmask * jax.nn.sigmoid(right[..., :hidden]) * right[..., hidden:]).astype(
        jnp.bfloat16
    )
    empty = jnp.zeros((rows, cols, hidden), jnp.float32)
    right_row = lax.all_gather(right_gated, "col", axis=1, tiled=True)
    right_mine = broadcast(right_row, "row", col_index)
    own_piece = lax.dynamic_slice_in_dim(right_mine, col_index * cols, cols, 1)
    start_total = outer_add(empty, left_gated, own_piece)

    def cannon_turn(turn, carry):
        moving, running = carry
        moving = from_behind(moving, "col", 1)
        source = (col_index - turn) % width
        piece = lax.dynamic_slice_in_dim(right_mine, source * cols, cols, 1)
        return (moving, outer_add(running, moving, piece))

    spent, product = lax.fori_loop(1, width, cannon_turn, (left_gated, start_total))
    ohat, oinv = apply_layer_norm(product)
    mid = (ohat * mid_gain + mid_bias).astype(jnp.bfloat16)
    value = jnp.dot(
        mid.reshape(rows * cols, hidden), proj_out, preferred_element_type=jnp.float32
    ).reshape(rows, cols, chans)
    gate = jax.nn.sigmoid(jnp.dot(flat, gate_out, preferred_element_type=jnp.float32)).reshape(
        rows, cols, chans
    )
    update = (gate * value).astype(jnp.bfloat16)
    upstream = cotangent.astype(jnp.float32)
    grad_value = (upstream * gate).astype(jnp.bfloat16)
    grad_gpre = (upstream * value * gate * (1.0 - gate)).astype(jnp.bfloat16)
    grad_mid = jnp.dot(
        grad_value.reshape(rows * cols, chans), proj_out.T, preferred_element_type=jnp.float32
    ).reshape(rows, cols, hidden)
    grad_product = layer_norm_backward(grad_mid * mid_gain, ohat, oinv).astype(jnp.bfloat16)
    grad_column, left_column, right_column = (
        lax.all_gather(grad_product, "row", axis=0, tiled=True),
        lax.all_gather(left_gated, "row", axis=0, tiled=True),
        lax.all_gather(right_gated, "row", axis=0, tiled=True),
    )
    grad_lg = jnp.einsum(
        "ijc,jkc->ikc",
        lax.all_gather(grad_product, "col", axis=1, tiled=True),
        right_column,
        preferred_element_type=jnp.float32,
    )
    grad_mine = broadcast(grad_column, "col", row_index)
    grad_rg = jnp.einsum("ijc,ikc->jkc", grad_mine, left_column, preferred_element_type=jnp.float32)
    dleft = gating_back(grad_lg, left, pmask, hidden).reshape(rows * cols, 2 * hidden)
    dright = gating_back(grad_rg, right, pmask, hidden).reshape(rows * cols, 2 * hidden)
    normalized_gradient = jnp.dot(dleft, proj_left.T, preferred_element_type=jnp.float32)
    normalized_gradient = normalized_gradient + jnp.dot(
        dright, proj_right.T, preferred_element_type=jnp.float32
    )
    normalized_gradient = normalized_gradient + jnp.dot(
        grad_gpre.reshape(rows * cols, chans), gate_out.T, preferred_element_type=jnp.float32
    )
    normalized_gradient = normalized_gradient.reshape(rows, cols, chans)
    bias_sum, gain_sum = lax.psum(
        (
            jnp.sum(normalized_gradient, axis=(0, 1)),
            jnp.sum(normalized_gradient * standardized_input, axis=(0, 1)),
        ),
        ("row", "col"),
    )
    grad_bias = bias_sum / total_res
    gain_gradient = gain_sum / total_res
    pair_gradient = layer_norm_backward(
        normalized_gradient * input_norm_gain, standardized_input, reciprocal_deviation
    )
    return (update, pair_gradient, gain_gradient, grad_bias)


def solution(mesh):
    return jax.shard_map(
        on_device,
        mesh=mesh,
        in_specs=(
            P(("groups", "row"), "col", None),
            P("groups"),
            P(),
            P(),
            P(),
            P(),
            P(),
            P(),
            P(),
            P(),
            P(("groups", "row"), "col", None),
        ),
        out_specs=(
            P(("groups", "row"), "col", None),
            P(("groups", "row"), "col", None),
            P("groups"),
            P("groups"),
        ),
        check_vma=False,
    )
```

profile of v0, /device:TPU:0, one launch (start us, length us, event | category | flops | bytes accessed | tf_op | source)
XLA Modules:
  0.0 214.6 jit_solution(10282534751674291035)
XLA Ops:
  7.2 0.7 convert_element_type.39
  7.9 0.9 convert_reduce_fusion
  11.7 15.6 %all_gather.15 = bf16[16,64,128]{2,1,0:T(8,128)(2,1)S(1)} all-gather(bf16[16,16,128]{2,1,0:T(8,128)(2,1)S(1)} %get-tuple-element.179), channel_id=1, replica_groups=mesh['groups'=2,'row'=4,'col'=4] {'col'}, dimensions={1}, use_global_device_ids=true | all-gather | bytes 327680 | tf_op jit(solution)/shard_map/all_gather | solution.py:84
  27.3 0.7 broadcast_select_fusion.1
  28.1 5.8 %all_gather.16 = bf16[64,16,128]{2,1,0:T(8,128)(2,1)S(1)} all-gather(bf16[16,16,128]{2,1,0:T(8,128)(2,1)S(1)} %get-tuple-element.179), channel_id=1, replica_groups=mesh['groups'=2,'row'=4,'col'=4] {'row'}, dimensions={0}, use_global_device_ids=true | all-gather | bytes 327680 | tf_op jit(solution)/shard_map/all_gather | solution.py:116
  33.9 1.2 copy.46
  35.1 6.4 %all_gather.18 = bf16[64,16,128]{2,1,0:T(8,128)(2,1)S(1)} all-gather(bf16[16,16,128]{2,1,0:T(8,128)(2,1)S(1)} %get-tuple-element.180), channel_id=1, replica_groups=mesh['groups'=2,'row'=4,'col'=4] {'row'}, dimensions={0}, use_global_device_ids=true | all-gather | bytes 327680 | tf_op jit(solution)/shard_map/all_gather | solution.py:115
  41.4 1.3 copy.50
  43.7 18.3 %all-reduce.4.cloned.1.call-done = bf16[16,64,128]{2,1,0:T(8,128)(2,1)} async-done(((bf16[16,64,128]{2,1,0:T(8,128)(2,1)}), bf16[16,64,128]{2,1,0:T(8,128)(2,1)}) %all-reduce.4.cloned.1.call-update) | async-done | bytes 262160 | tf_op jit(solution)/shard_map/psum | solution.py:9
  62.0 0.8 constant_dynamic-slice_fusion.1
  63.2 1.4 convolution_bitcast_fusion.1
  64.7 44.0 %while.17 = (s32[]{:T(128)}, bf16[16,16,128]{1,0,2:T(8,128)(2,1)}, f32[16,16,128]{0,1,2:T(8,128)S(1)}, s32[]{:T(128)}, bf16[16,64,128]{2,1,0:T(8,128)(2,1)}, /*i...) while((s32[]{:T(128)}, bf16[16,16,128]{1,0,2:T(8,128)(2,1)}, ...), condition=%wide.region_4.5_spmd, body=%wide.region_3.4_spmd.sunk | while | flops 1081362 | bytes 1048896 | solution.py:96
  64.7 1.5 collective-permute-start
  66.2 0.8 constant_dynamic-slice_fusion.3
  67.5 11.6 %collective-permute-done = bf16[16,16,128]{1,0,2:T(8,128)(2,1)S(1)} collective-permute-done((bf16[16,16,128]{1,0,2:T(8,128)(2,1)}, bf16[16,16,128]{1,0,2:T(8,128)(2,1)S(1)}, u32[]{:S(2)}, u32[]{:S(2)}) %collective-permute-start) | collective-permute-done | bytes 65568 | tf_op jit(solution)/shard_map/while/body/eval_jaxpr/ppermute | solution.py:15
  79.1 0.8 copy.67
  80.4 0.9 constant_dynamic-slice_fusion.3
  81.7 12.1 %collective-permute-done = bf16[16,16,128]{1,0,2:T(8,128)(2,1)S(1)} collective-permute-done((bf16[16,16,128]{1,0,2:T(8,128)(2,1)}, bf16[16,16,128]{1,0,2:T(8,128)(2,1)S(1)}, u32[]{:S(2)}, u32[]{:S(2)}) %collective-permute-start) | collective-permute-done | bytes 65568 | tf_op jit(solution)/shard_map/while/body/eval_jaxpr/ppermute | solution.py:15
  93.7 0.8 copy.67
  95.0 0.9 constant_dynamic-slice_fusion.3
  96.3 11.2 %collective-permute-done = bf16[16,16,128]{1,0,2:T(8,128)(2,1)S(1)} collective-permute-done((bf16[16,16,128]{1,0,2:T(8,128)(2,1)}, bf16[16,16,128]{1,0,2:T(8,128)(2,1)S(1)}, u32[]{:S(2)}, u32[]{:S(2)}) %collective-permute-start) | collective-permute-done | bytes 65568 | tf_op jit(solution)/shard_map/while/body/eval_jaxpr/ppermute | solution.py:15
  107.5 0.8 copy.67
  110.8 14.2 %all_gather.17 = bf16[16,64,128]{2,1,0:T(8,128)(2,1)S(1)} all-gather(bf16[16,16,128]{2,1,0:T(8,128)(2,1)S(1)} %multiply_convert_fusion.4), channel_id=1, replica_groups=mesh['groups'=2,'row'=4,'col'=4] {'col'}, dimensions={1}, use_global_device_ids=true | all-gather | bytes 327680 | tf_op jit(solution)/shard_map/all_gather | solution.py:120
  125.0 7.0 %all_gather.19 = bf16[64,16,128]{2,1,0:T(8,128)(2,1)S(1)} all-gather(bf16[16,16,128]{2,1,0:T(8,128)(2,1)S(1)} %multiply_convert_fusion.4), channel_id=1, replica_groups=mesh['groups'=2,'row'=4,'col'=4] {'row'}, dimensions={0}, use_global_device_ids=true | all-gather | bytes 327680 | tf_op jit(solution)/shard_map/all_gather | solution.py:114
  133.0 0.8 broadcast_select_fusion
  133.8 1.0 copy-done.1
  135.7 0.9 fusion.21
  137.5 32.5 %all-reduce.6.cloned.1.call-done = bf16[64,16,128]{0,1,2:T(8,128)(2,1)} async-done(((bf16[64,16,128]{0,1,2:T(8,128)(2,1)}), bf16[64,16,128]{0,1,2:T(8,128)(2,1)}) %all-reduce.6.cloned.1.call-update) | async-done | bytes 262160 | tf_op jit(solution)/shard_map/psum | solution.py:9
  170.0 1.4 fusion.53
  172.3 0.7 copy-done.4
  174.7 31.1 %all-reduce = (f32[128]{0:T(128)S(1)}, f32[128]{0:T(128)S(1)}) all-reduce(f32[128]{0:T(128)S(1)} %get-tuple-element.157, f32[128]{0:T(128)S(1)} %get-tuple-element.153), channel_id=1, replica_groups=mesh['groups'=2,'row'=4,'col'=4] {'row','col'}, use_global_device_ids=true, to_apply=%region_13.14 | all-reduce | flops 256 | bytes 2048 | tf_op jit(solution)/shard_map/psum | solution.py:136
  206.9 0.9 fusion.15
  (92 shorter events, 15.2 us)
Async XLA Ops:
  7.2 2.7 %copy-start = (bf16[128,256]{1,0:T(8,128)(2,1)S(1)}, bf16[128,256]{1,0:T(8,128)(2,1)}, u32[]{:S(2)}) copy-start(bf16[128,256]{1,0:T(8,128)(2,1)} %param.18) | copy-start | bytes 196612
  7.2 1.7 copy-start.2
  7.2 54.8 %all-reduce.4.cloned.1.call-start = ((), (), s32[]{:S(2)}) async-start(), calls=%async_computation | async-start | bytes 524288 | tf_op jit(solution)/shard_map/psum | solution.py:9
  9.1 0.7 copy-start.17
  9.1 0.7 copy-start.21
  9.1 0.6 copy-start.11
  9.9 0.8 copy-start.3
  11.1 0.6 copy-start.13
  28.0 141.9 %all-reduce.6.cloned.1.call-start = ((), (), s32[]{:S(2)}) async-start(), calls=%async_computation.1 | async-start | bytes 1048576 | tf_op jit(solution)/shard_map/psum | solution.py:9
  42.7 0.8 copy-start.15
  64.7 14.4 %collective-permute-start = (bf16[16,16,128]{1,0,2:T(8,128)(2,1)}, bf16[16,16,128]{1,0,2:T(8,128)(2,1)S(1)}, u32[]{:S(2)}, u32[]{:S(2)}) collective-permute-start(bf16[16,16,128]{1,0,2:T(8,128)(2,1)} %get-tuple-element.230), channel_id=1, source_target_pairs={{0,1},{1,2},{2,3},{3,0},{4,5},{5,6},{6,7},{7,4},{8,9},{9,10},{10,1... | collective-permute-start | bytes 196616 | tf_op jit(solution)/shard_map/while/body/eval_jaxpr/ppermute | solution.py:15
  80.3 13.5 %collective-permute-start = (bf16[16,16,128]{1,0,2:T(8,128)(2,1)}, bf16[16,16,128]{1,0,2:T(8,128)(2,1)S(1)}, u32[]{:S(2)}, u32[]{:S(2)}) collective-permute-start(bf16[16,16,128]{1,0,2:T(8,128)(2,1)} %get-tuple-element.230), channel_id=1, source_target_pairs={{0,1},{1,2},{2,3},{3,0},{4,5},{5,6},{6,7},{7,4},{8,9},{9,10},{10,1... | collective-permute-start | bytes 196616 | tf_op jit(solution)/shard_map/while/body/eval_jaxpr/ppermute | solution.py:15
  94.9 12.5 %collective-permute-start = (bf16[16,16,128]{1,0,2:T(8,128)(2,1)}, bf16[16,16,128]{1,0,2:T(8,128)(2,1)S(1)}, u32[]{:S(2)}, u32[]{:S(2)}) collective-permute-start(bf16[16,16,128]{1,0,2:T(8,128)(2,1)} %get-tuple-element.230), channel_id=1, source_target_pairs={{0,1},{1,2},{2,3},{3,0},{4,5},{5,6},{6,7},{7,4},{8,9},{9,10},{10,1... | collective-permute-start | bytes 196616 | tf_op jit(solution)/shard_map/while/body/eval_jaxpr/ppermute | solution.py:15
  109.1 0.8 copy-start.9
  109.4 0.8 copy-start.5
  109.6 1.0 copy-start.7
  109.6 0.7 copy-start.19
  133.8 1.0 copy-start.1
  134.8 0.8 copy-start.6
  134.8 0.8 copy-start.8
  134.9 0.8 copy-start.10
  134.9 0.8 copy-start.20
  134.9 0.8 copy-start.22
  136.6 0.8 copy-start.16
  171.4 0.7 copy-start.14
  172.1 0.8 copy-start.4
  173.1 0.7 copy-start.18
  173.8 0.7 copy-start.12
Sparse Core Ops, SparseCore 0:
  28.2 33.7 all-reduce.3
  134.0 35.9 all-reduce.5
where the time goes:
time: 216 us; the launch traced here: 215 us
  waiting for transfers between devices  85.6 us (40%)
  blocking collectives  80 us (37%)
  local copies, waits for them, and re-layouts  19.5 us (9%)
  between operations  14.4 us (7%)
  matrix products  6.7 us (3%)
  other arithmetic  6.52 us (3%)
    psum x2, waiting for transfers between devices, broadcast(): return lax.psum(jnp.where(mine, array, jnp.zeros_like(array)), axis)  50.8 us
    ppermute x3, waiting for transfers between devices, from_behind(): return lax.ppermute(value, axis, pairs)  34.8 us
    psum x1, blocking collectives, on_device(): lax.psum((jnp.sum(normalized_gradient, axis=(0, 1)), jnp.sum(normalized_g...  31.1 us
    all_gather x1, blocking collectives, on_device(): right_row = lax.all_gather(right_gated, 'col', axis=1, tiled=True)  15.6 us
    all_gather x1, blocking collectives, on_device(): lax.all_gather(grad_product, 'col', axis=1, tiled=True)  14.2 us
    all_gather x1, blocking collectives, on_device(): lax.all_gather(grad_product, 'row', axis=0, tiled=True)  6.96 us
    unnamed x46, local copies, waits for them, and re-layouts  6.5 us
    all_gather x1, blocking collectives, on_device(): lax.all_gather(left_gated, 'row', axis=0, tiled=True)  6.38 us
  transfers between devices with their start and end apart: 5, of which 5 were waited for; matrix products, arithmetic and copies ran while one was open for 4% of the time, Pallas kernels for 0%

commit v1 on v0

v1 whole, which is shorter than its diff:
```python
import functools

import jax
import jax.numpy as jnp
from jax import lax
from jax.experimental import pallas as pl
from jax.experimental.pallas import tpu as pltpu
from jax.sharding import PartitionSpec as P

MESH = pl.DeviceIdType.MESH
F32 = jnp.float32
BF16 = jnp.bfloat16


def normalize(values):
    center = values - jnp.mean(values, axis=-1, keepdims=True)
    inverse = lax.rsqrt(jnp.mean(center * center, axis=-1, keepdims=True) + 1e-05)
    return center * inverse, inverse


def normalize_backward(grad_hat, hatted, inverse):
    first = jnp.mean(grad_hat, axis=-1, keepdims=True)
    second = jnp.mean(grad_hat * hatted, axis=-1, keepdims=True)
    return (grad_hat - first - hatted * second) * inverse


def dot(a, b):
    return jnp.dot(a, b, preferred_element_type=F32)


def dot_transposed(a, b):
    return lax.dot_general(a, b, (((1,), (1,)), ((), ())), preferred_element_type=F32)


def loop(low, high, body):
    if high - low <= 4:
        for step in range(low, high):
            body(step)
    else:
        lax.fori_loop(low, high, lambda step, _: (body(step), 0)[1], 0)


def kernel(
    side,
    pair_ref,
    mask_ref,
    gain_ref,
    bias_ref,
    pl_ref,
    pr_ref,
    go_ref,
    mgain_ref,
    mbias_ref,
    po_ref,
    cot_ref,
    update_ref,
    pgrad_ref,
    ggrad_ref,
    bgrad_ref,
    right_all,
    right32,
    left32,
    part_send,
    part_recv,
    grad_all,
    grad32,
    lg_sum,
    q_send,
    q_recv,
    stat_send,
    stat_recv,
    right_ssem,
    right_rsem,
    part_ssem,
    part_rsem,
    grad_ssem,
    grad_rsem,
    q_ssem,
    q_rsem,
    stat_ssem,
    stat_rsem,
):
    rows, cols, chans = pair_ref.shape
    pairs = rows * cols
    hidden = pl_ref.shape[1] // 2
    total = mask_ref.shape[1]
    peers = side * side
    row = lax.axis_index("row")
    col = lax.axis_index("col")
    me = row * side + col

    def device(r, c):
        return {"row": r, "col": c}

    barrier = pltpu.get_barrier_semaphore()

    def greet(step):
        other = me ^ step
        pl.semaphore_signal(
            barrier, inc=1, device_id=device(other // side, other % side), device_id_type=MESH
        )

    if peers <= 16:
        for step in range(1, peers):
            greet(step)
    else:
        lax.fori_loop(1, peers, lambda step, _: (greet(step), 0)[1], 0)

    xhat, inverse = normalize(pair_ref[...].reshape(pairs, chans).astype(F32))
    normed = (xhat * gain_ref[...] + bias_ref[...]).astype(BF16)

    spot = lax.broadcasted_iota(jnp.int32, (pairs, total), 0)
    lane = lax.broadcasted_iota(jnp.int32, (pairs, total), 1)
    maskf = mask_ref[...].astype(F32)
    mask_row = jnp.sum(
        jnp.where(lane == row * rows + spot // cols, maskf, 0.0), axis=-1, keepdims=True
    )
    mask_col = jnp.sum(
        jnp.where(lane == col * cols + spot % cols, maskf, 0.0), axis=-1, keepdims=True
    )
    pmask = mask_row * mask_col

    right = dot(normed, pr_ref[...])
    right_sig = jax.nn.sigmoid(right[:, :hidden])
    right_val = right[:, hidden:]
    right_all[row] = (pmask * right_sig * right_val).astype(BF16)

    pl.semaphore_wait(barrier, peers - 1)

    def right_copy(step):
        return pltpu.make_async_remote_copy(
            src_ref=right_all.at[row],
            dst_ref=right_all.at[row],
            send_sem=right_ssem.at[step],
            recv_sem=right_rsem.at[step],
            device_id=device(row ^ step, col),
            device_id_type=MESH,
        )

    loop(1, side, lambda step: right_copy(step).start())

    left = dot(normed, pl_ref[...])
    left_sig = jax.nn.sigmoid(left[:, :hidden])
    left_val = left[:, hidden:]
    left_gated = (pmask * left_sig * left_val).astype(BF16).astype(F32)
    left32[...] = left_gated.reshape(rows, cols, hidden)
    gate = jax.nn.sigmoid(dot(normed, go_ref[...]))

    def part_copy(slot, r, c, sem):
        return pltpu.make_async_remote_copy(
            src_ref=part_send.at[slot],
            dst_ref=part_recv.at[col],
            send_sem=part_ssem.at[sem],
            recv_sem=part_rsem.at[sem],
            device_id=device(r, c),
            device_id_type=MESH,
        )

    def product_block(step):
        block = row ^ step
        if not (isinstance(step, int) and step == 0):
            right_copy(step).wait_recv()
        base = pl.multiple_of(block * pairs, pairs)
        right32[pl.ds(base, pairs), :] = right_all[block].astype(F32)
        acc = None
        for k in range(cols):
            term = left32[:, k : k + 1, :] * right32[pl.ds(base + k, rows, stride=cols), :][None]
            acc = term if acc is None else acc + term
        part_send[block] = acc.reshape(pairs, hidden).astype(BF16)

        @pl.when(block != col)
        def _():
            part_copy(block, row, block, col ^ block).start()

    product_block(0)
    loop(1, side, product_block)

    held = [part_send[col].astype(F32)]

    if side <= 4:
        product = part_send[col].astype(F32)
        for step in range(1, side):
            part_copy(0, row, col ^ step, step).wait_recv()
            product = product + part_recv[col ^ step].astype(F32)
    else:

        def add_part(step, running):
            part_copy(0, row, col ^ step, step).wait_recv()
            return running + part_recv[col ^ step].astype(F32)

        product = lax.fori_loop(1, side, add_part, held[0])

    ohat, oinv = normalize(product)
    mid = (ohat * mgain_ref[...] + mbias_ref[...]).astype(BF16)
    value = dot(mid, po_ref[...])
    upstream = cot_ref[...].reshape(pairs, chans).astype(F32)
    grad_value = (upstream * gate).astype(BF16)
    grad_mid = dot_transposed(grad_value, po_ref[...])
    grad_product = normalize_backward(grad_mid * mgain_ref[...], ohat, oinv)
    grad_all[col] = grad_product.astype(BF16)

    def grad_copy(step):
        return pltpu.make_async_remote_copy(
            src_ref=grad_all.at[col],
            dst_ref=grad_all.at[col],
            send_sem=grad_ssem.at[step],
            recv_sem=grad_rsem.at[step],
            device_id=device(row, col ^ step),
            device_id_type=MESH,
        )

    loop(1, side, lambda step: grad_copy(step).start())

    update_ref[...] = (gate * value).astype(BF16).reshape(rows, cols, chans)
    grad_gpre = (upstream * value * gate * (1.0 - gate)).astype(BF16)

    def q_copy(slot, r, sem):
        return pltpu.make_async_remote_copy(
            src_ref=q_send.at[slot],
            dst_ref=q_recv.at[row],
            send_sem=q_ssem.at[sem],
            recv_sem=q_rsem.at[sem],
            device_id=device(r, col),
            device_id_type=MESH,
        )

    lg_sum[...] = jnp.zeros_like(lg_sum)

    def grad_block(step):
        block = col ^ step
        if not (isinstance(step, int) and step == 0):
            grad_copy(step).wait_recv()
        grad32[...] = grad_all[block].astype(F32).reshape(rows, cols, hidden)
        for j in range(cols):
            term = jnp.sum(grad32[:, j : j + 1, :] * left32[...], axis=0)
            q_send[block, j * cols : (j + 1) * cols, :] = term.astype(BF16)

        @pl.when(block != row)
        def _():
            q_copy(block, block, row ^ block).start()

        acc = lg_sum[...]
        base = pl.multiple_of(block * pairs, pairs)
        for j in range(cols):
            acc = acc + grad32[:, j : j + 1, :] * right32[pl.ds(base + j * cols, cols), :][None]
        lg_sum[...] = acc

    grad_block(0)
    loop(1, side, grad_block)

    def gating_back(grad_out, sig, val):
        masked = grad_out * pmask
        return jnp.concatenate([masked * val * sig * (1.0 - sig), masked * sig], axis=-1).astype(
            BF16
        )

    dleft = gating_back(lg_sum[...].reshape(pairs, hidden), left_sig, left_val)
    normalized_gradient = dot_transposed(dleft, pl_ref[...]) + dot_transposed(
        grad_gpre, go_ref[...]
    )

    def add_q(step, running):
        q_copy(0, row ^ step, step).wait_recv()
        return running + q_recv[row ^ step].astype(F32)

    grad_rg = q_send[row].astype(F32)
    if side <= 4:
        for step in range(1, side):
            grad_rg = add_q(step, grad_rg)
    else:
        grad_rg = lax.fori_loop(1, side, add_q, grad_rg)
    dright = gating_back(grad_rg, right_sig, right_val)
    normalized_gradient = normalized_gradient + dot_transposed(dright, pr_ref[...])

    stat_send[0:1, :] = jnp.sum(normalized_gradient, axis=0, keepdims=True)
    stat_send[1:2, :] = jnp.sum(normalized_gradient * xhat, axis=0, keepdims=True)

    def stat_copy(step):
        other = me ^ step
        return pltpu.make_async_remote_copy(
            src_ref=stat_send,
            dst_ref=stat_recv.at[step - 1],
            send_sem=stat_ssem,
            recv_sem=stat_rsem,
            device_id=device(other // side, other % side),
            device_id_type=MESH,
        )

    if peers <= 16:
        for step in range(1, peers):
            stat_copy(step).start()
    else:
        lax.fori_loop(1, peers, lambda step, _: (stat_copy(step).start(), 0)[1], 0)

    pgrad_ref[...] = normalize_backward(
        normalized_gradient * gain_ref[...], xhat, inverse
    ).reshape(rows, cols, chans)

    def sent(step):
        right_copy(step).wait_send()
        part_copy(0, row, col ^ step, step).wait_send()
        grad_copy(step).wait_send()
        q_copy(0, row ^ step, step).wait_send()

    loop(1, side, sent)
    pltpu.make_async_copy(stat_recv, stat_recv, stat_rsem).wait()
    stats = stat_send[...] + jnp.sum(stat_recv[...], axis=0)
    bgrad_ref[...] = stats[0:1, :] / total
    ggrad_ref[...] = stats[1:2, :] / total
    pltpu.make_async_copy(stat_recv, stat_recv, stat_ssem).wait()


def on_device(
    side,
    pair,
    res_mask,
    input_norm_gain,
    input_norm_bias,
    proj_left,
    proj_right,
    gate_out,
    mid_gain,
    mid_bias,
    proj_out,
    cotangent,
):
    rows, cols, chans = pair.shape
    hidden = proj_left.shape[1] // 2
    pairs = rows * cols
    blocks = (side, pairs, hidden)
    vmem = pl.BlockSpec(memory_space=pltpu.VMEM)
    update, pair_gradient, gain_gradient, grad_bias = pl.pallas_call(
        functools.partial(kernel, side),
        out_shape=(
            jax.ShapeDtypeStruct((rows, cols, chans), BF16),
            jax.ShapeDtypeStruct((rows, cols, chans), F32),
            jax.ShapeDtypeStruct((1, chans), F32),
            jax.ShapeDtypeStruct((1, chans), F32),
        ),
        in_specs=[vmem] * 11,
        out_specs=(vmem,) * 4,
        scratch_shapes=[
            pltpu.VMEM(blocks, BF16),
            pltpu.VMEM((side * pairs, hidden), F32),
            pltpu.VMEM((rows, cols, hidden), F32),
            pltpu.VMEM(blocks, BF16),
            pltpu.VMEM(blocks, BF16),
            pltpu.VMEM(blocks, BF16),
            pltpu.VMEM((rows, cols, hidden), F32),
            pltpu.VMEM((rows, cols, hidden), F32),
            pltpu.VMEM(blocks, BF16),
            pltpu.VMEM(blocks, BF16),
            pltpu.VMEM((2, chans), F32),
            pltpu.VMEM((side * side - 1, 2, chans), F32),
        ]
        + [pltpu.SemaphoreType.DMA((side,))] * 8
        + [pltpu.SemaphoreType.DMA] * 2,
        compiler_params=pltpu.CompilerParams(
            collective_id=0, has_side_effects=True, vmem_limit_bytes=40 * 1024 * 1024
        ),
        name="triangle",
    )(
        pair,
        res_mask.reshape(1, -1),
        input_norm_gain.reshape(1, -1),
        input_norm_bias.reshape(1, -1),
        proj_left,
        proj_right,
        gate_out,
        mid_gain.reshape(1, -1),
        mid_bias.reshape(1, -1),
        proj_out,
        cotangent,
    )
    return update, pair_gradient, gain_gradient.reshape(-1), grad_bias.reshape(-1)


def solution(mesh):
    blocks = P(("groups", "row"), "col", None)
    return jax.shard_map(
        functools.partial(on_device, mesh.shape["row"]),
        mesh=mesh,
        in_specs=(blocks, P("groups")) + (P(),) * 8 + (blocks,),
        out_specs=(blocks, blocks, P("groups"), P("groups")),
        check_vma=False,
    )
```

time: 216 us -> 42.4 us (0.20)
  waiting for transfers between devices: 85.6 us -> 0 us
  blocking collectives: 80 us -> 0 us
  Pallas kernels: 0 us -> 33.4 us
  between operations: 14.4 us -> 0.69 us
  local copies, waits for them, and re-layouts: 19.5 us -> 7.86 us
  matrix products: 6.7 us -> 0 us
  other arithmetic: 6.52 us -> 0 us
    psum x2 -> x0, waiting for transfers between devices: 50.8 us -> none  [broadcast(): return lax.psum(jnp.where(mine, array, jnp.zeros_like(array)), axis)]
    all_gather x5 -> x0, blocking collectives: 49 us -> none  [the longest x1 15.6 us: on_device(): right_row = lax.all_gather(right_gated, 'col', axis=1, tiled=True)]
    ppermute x3 -> x0, waiting for transfers between devices: 34.8 us -> none  [from_behind(): return lax.ppermute(value, axis, pairs)]
    pallas_call x0 -> x1, Pallas kernels: none -> 33.4 us  [on_device(): pl.pallas_call(functools.partial(kernel, side), out_shape=(jax.ShapeDtype...]
    psum x1 -> x0, blocking collectives: 31.1 us -> none  [on_device(): lax.psum((jnp.sum(normalized_gradient, axis=(0, 1)), jnp.sum(normalized_g...]
    dot_general x14 -> x0, matrix products: 6.7 us -> none  [the longest x4 2.63 us: outer_add(): jnp.einsum('ikc,jkc->ijc', left_block, right_block, preferred_element_typ...]
    dynamic_slice x9 -> x0, local copies, waits for them, and re-layouts: 5.18 us -> none  [the longest x6 3.83 us: cannon_turn(): piece = lax.dynamic_slice_in_dim(right_mine, source * cols, cols, 1)]
    while x5 -> x0, local copies, waits for them, and re-layouts: 4 us -> none
  transfers between devices with their start and end apart: 5 -> 0, of which waited for: 5 -> 0; matrix products, arithmetic and copies ran while one was open for 4% -> 0% of each run, Pallas kernels for 0% -> 0%
where the time goes in v1:
time: 42.4 us; the launch traced here: 41.9 us
  Pallas kernels  33.4 us (79%)
  local copies, waits for them, and re-layouts  7.86 us (19%)
  between operations  0.69 us (2%)
    pallas_call x1, Pallas kernels, on_device(): pl.pallas_call(functools.partial(kernel, side), out_shape=(jax.ShapeDtype...  33.4 us
    unnamed x26, local copies, waits for them, and re-layouts  7.86 us

profile of v1, /device:TPU:0, one launch (start us, length us, event | category | flops | bytes accessed | tf_op | source)
XLA Modules:
  0.0 41.9 jit_solution(6474358348562379497)
XLA Ops:
  0.6 0.0 copy-start.9
  0.6 0.0 copy-start.10
  0.7 0.0 copy-start.6
  0.7 0.0 copy-start.7
  0.7 0.0 copy-start.8
  0.7 0.6 %copy-done.9 = f32[128]{0:T(128)S(1)} copy-done((f32[128]{0:T(128)S(1)}, f32[128]{0:T(128)}, u32[]{:S(2)}) %copy-start.9) | copy-done | bytes 536
  1.3 0.0 copy-done.10
  1.3 0.0 copy-done.6
  1.3 0.0 copy-done.7
  1.3 0.0 copy-done.8
  1.4 0.0 copy-start
  1.4 0.8 %copy-done = bf16[16,16,128]{2,1,0:T(8,128)(2,1)S(1)} copy-done((bf16[16,16,128]{2,1,0:T(8,128)(2,1)S(1)}, bf16[16,16,128]{2,1,0:T(8,128)(2,1)}, u32[]{:S(2)}) %copy-start) | copy-done | bytes 65560
  2.2 0.0 copy-start.1
  2.2 0.8 %copy-done.1 = bf16[128,256]{1,0:T(8,128)(2,1)S(1)} copy-done((bf16[128,256]{1,0:T(8,128)(2,1)S(1)}, bf16[128,256]{1,0:T(8,128)(2,1)}, u32[]{:S(2)}) %copy-start.1) | copy-done | bytes 65560
  3.0 0.0 copy-start.2
  3.0 0.8 %copy-done.2 = bf16[128,256]{1,0:T(8,128)(2,1)S(1)} copy-done((bf16[128,256]{1,0:T(8,128)(2,1)S(1)}, bf16[128,256]{1,0:T(8,128)(2,1)}, u32[]{:S(2)}) %copy-start.2) | copy-done | bytes 65560
  3.9 0.0 copy-start.3
  3.9 0.8 %copy-done.3 = bf16[16,16,128]{2,1,0:T(8,128)(2,1)S(1)} copy-done((bf16[16,16,128]{2,1,0:T(8,128)(2,1)S(1)}, bf16[16,16,128]{2,1,0:T(8,128)(2,1)}, u32[]{:S(2)}) %copy-start.3) | copy-done | bytes 65560
  4.7 0.0 copy-start.4
  4.7 0.8 %copy-done.4 = bf16[128,128]{1,0:T(8,128)(2,1)S(1)} copy-done((bf16[128,128]{1,0:T(8,128)(2,1)S(1)}, bf16[128,128]{1,0:T(8,128)(2,1)}, u32[]{:S(2)}) %copy-start.4) | copy-done | bytes 32792
  5.5 0.0 copy-start.5
  5.5 0.8 %copy-done.5 = bf16[128,128]{1,0:T(8,128)(2,1)S(1)} copy-done((bf16[128,128]{1,0:T(8,128)(2,1)S(1)}, bf16[128,128]{1,0:T(8,128)(2,1)}, u32[]{:S(2)}) %copy-start.5) | copy-done | bytes 32792
  6.2 33.4 %triangle.1 = (bf16[16,16,128]{2,1,0:T(8,128)(2,1)S(1)}, f32[16,16,128]{2,1,0:T(8,128)S(1)}, f32[1,128]{1,0:T(1,128)S(1)}, f32[1,128]{1,0:T(1,128)S(1)}) custom-call(bf16[16,16,128]{2,1,0:T(8,128)(2,1)S(1)} %copy-done, s32[1,64]{1,0:T(1,128)S(1)} %bitcast.7, f32[1,128]{1,0:T(1,128)S(1)} %bitcast.8, f32[1,128]{1,0:T(1,128)S(1)} %bitcast.9, ...), custom_call_target="tpu_custom_call" | custom-call | tf_op jit(solution)/shard_map/triangle/pallas_call | solution.py:332
  39.6 0.6 %copy.19 = bf16[16,16,128]{2,1,0:T(8,128)(2,1)} copy(bf16[16,16,128]{2,1,0:T(8,128)(2,1)S(1)} %get-tuple-element.16) | data formatting | bytes 131072
  40.2 0.7 %copy.20 = f32[16,16,128]{2,1,0:T(8,128)} copy(f32[16,16,128]{2,1,0:T(8,128)S(1)} %get-tuple-element.17) | data formatting | bytes 262144
  40.9 0.5 %copy.21 = f32[128]{0:T(128)} copy(f32[128]{0:T(128)S(1)} %bitcast.13) | data formatting | bytes 1024
  41.4 0.5 %copy.22 = f32[128]{0:T(128)} copy(f32[128]{0:T(128)S(1)} %bitcast.12) | data formatting | bytes 1024
Async XLA Ops:
  0.6 0.7 %copy-start.9 = (f32[128]{0:T(128)S(1)}, f32[128]{0:T(128)}, u32[]{:S(2)}) copy-start(f32[128]{0:T(128)} %param.18) | copy-start | bytes 1540
  0.6 0.7 %copy-start.10 = (f32[128]{0:T(128)S(1)}, f32[128]{0:T(128)}, u32[]{:S(2)}) copy-start(f32[128]{0:T(128)} %param.19) | copy-start | bytes 1540
  0.7 0.7 %copy-start.6 = (s32[64]{0:T(128)S(1)}, s32[64]{0:T(128)}, u32[]{:S(2)}) copy-start(s32[64]{0:T(128)} %param.12) | copy-start | bytes 772
  0.7 0.7 %copy-start.7 = (f32[128]{0:T(128)S(1)}, f32[128]{0:T(128)}, u32[]{:S(2)}) copy-start(f32[128]{0:T(128)} %param.13) | copy-start | bytes 1540
  0.7 0.7 %copy-start.8 = (f32[128]{0:T(128)S(1)}, f32[128]{0:T(128)}, u32[]{:S(2)}) copy-start(f32[128]{0:T(128)} %param.14) | copy-start | bytes 1540
  1.4 0.8 %copy-start = (bf16[16,16,128]{2,1,0:T(8,128)(2,1)S(1)}, bf16[16,16,128]{2,1,0:T(8,128)(2,1)}, u32[]{:S(2)}) copy-start(bf16[16,16,128]{2,1,0:T(8,128)(2,1)} %pair_ref.1) | copy-start | bytes 196612
  2.2 0.8 %copy-start.1 = (bf16[128,256]{1,0:T(8,128)(2,1)S(1)}, bf16[128,256]{1,0:T(8,128)(2,1)}, u32[]{:S(2)}) copy-start(bf16[128,256]{1,0:T(8,128)(2,1)} %pl_ref.1) | copy-start | bytes 196612
  3.0 0.8 %copy-start.2 = (bf16[128,256]{1,0:T(8,128)(2,1)S(1)}, bf16[128,256]{1,0:T(8,128)(2,1)}, u32[]{:S(2)}) copy-start(bf16[128,256]{1,0:T(8,128)(2,1)} %pr_ref.1) | copy-start | bytes 196612
  3.9 0.8 %copy-start.3 = (bf16[16,16,128]{2,1,0:T(8,128)(2,1)S(1)}, bf16[16,16,128]{2,1,0:T(8,128)(2,1)}, u32[]{:S(2)}) copy-start(bf16[16,16,128]{2,1,0:T(8,128)(2,1)} %cot_ref.1) | copy-start | bytes 196612
  4.7 0.8 %copy-start.4 = (bf16[128,128]{1,0:T(8,128)(2,1)S(1)}, bf16[128,128]{1,0:T(8,128)(2,1)}, u32[]{:S(2)}) copy-start(bf16[128,128]{1,0:T(8,128)(2,1)} %go_ref.1) | copy-start | bytes 98308
  5.5 0.8 %copy-start.5 = (bf16[128,128]{1,0:T(8,128)(2,1)S(1)}, bf16[128,128]{1,0:T(8,128)(2,1)}, u32[]{:S(2)}) copy-start(bf16[128,128]{1,0:T(8,128)(2,1)} %po_ref.1) | copy-start | bytes 98308

commit v2 on v1

--- a/solution.py
+++ b/solution.py
@@ -10,6 +10,8 @@
 MESH = pl.DeviceIdType.MESH
 F32 = jnp.float32
 BF16 = jnp.bfloat16
+VMEM_LIMIT = 62 * 1024 * 1024
+HALVES = 2
 
 
 def normalize(values):
@@ -42,6 +44,23 @@
 
 def kernel(
     side,
+    pair_hbm,
+    mask_hbm,
+    gain_hbm,
+    bias_hbm,
+    pl_hbm,
+    pr_hbm,
+    go_hbm,
+    mgain_hbm,
+    mbias_hbm,
+    po_hbm,
+    cot_hbm,
+    update_hbm,
+    pgrad_hbm,
+    stats_hbm,
+    update_ref,
+    pgrad_ref,
+    stats_ref,
     pair_ref,
     mask_ref,
     gain_ref,
@@ -53,10 +72,8 @@
     mbias_ref,
     po_ref,
     cot_ref,
-    update_ref,
-    pgrad_ref,
-    ggrad_ref,
-    bgrad_ref,
+    load_sem,
+    store_sem,
     right_all,
     right32,
     left32,
@@ -65,6 +82,7 @@
     grad_all,
     grad32,
     lg_sum,
+    q_sum,
     q_send,
     q_recv,
     stat_send,
@@ -80,6 +98,27 @@
     stat_ssem,
     stat_rsem,
 ):
+    loads = [
+        pltpu.make_async_copy(source, target, load_sem.at[index])
+        for index, (source, target) in enumerate(
+            (
+                (pair_hbm, pair_ref),
+                (gain_hbm, gain_ref),
+                (bias_hbm, bias_ref),
+                (mask_hbm, mask_ref),
+                (pr_hbm, pr_ref),
+                (pl_hbm, pl_ref),
+                (go_hbm, go_ref),
+                (cot_hbm, cot_ref),
+                (po_hbm, po_ref),
+                (mgain_hbm, mgain_ref),
+                (mbias_hbm, mbias_ref),
+            )
+        )
+    ]
+    for load in loads:
+        load.start()
+
     rows, cols, chans = pair_ref.shape
     pairs = rows * cols
     hidden = pl_ref.shape[1] // 2
@@ -106,7 +145,10 @@
     else:
         lax.fori_loop(1, peers, lambda step, _: (greet(step), 0)[1], 0)
 
+    loads[0].wait()
     xhat, inverse = normalize(pair_ref[...].reshape(pairs, chans).astype(F32))
+    for load in loads[1:5]:
+        load.wait()
     normed = (xhat * gain_ref[...] + bias_ref[...]).astype(BF16)
 
     spot = lax.broadcasted_iota(jnp.int32, (pairs, total), 0)
@@ -139,6 +181,8 @@
 
     loop(1, side, lambda step: right_copy(step).start())
 
+    for load in loads[5:]:
+        load.wait()
     left = dot(normed, pl_ref[...])
     left_sig = jax.nn.sigmoid(left[:, :hidden])
     left_val = left[:, hidden:]
@@ -146,72 +190,108 @@
     left32[...] = left_gated.reshape(rows, cols, hidden)
     gate = jax.nn.sigmoid(dot(normed, go_ref[...]))
 
-    def part_copy(slot, r, c, sem):
+    part = pairs // HALVES
+    span = rows // HALVES
+
+    def part_copy(half, slot, c, step):
+        place = pl.ds(half * part, part)
         return pltpu.make_async_remote_copy(
-            src_ref=part_send.at[slot],
-            dst_ref=part_recv.at[col],
-            send_sem=part_ssem.at[sem],
-            recv_sem=part_rsem.at[sem],
-            device_id=device(r, c),
+            src_ref=part_send.at[slot, place],
+            dst_ref=part_recv.at[col, place],
+            send_sem=part_ssem.at[half, step],
+            recv_sem=part_rsem.at[half, step],
+            device_id=device(row, c),
             device_id_type=MESH,
         )
 
-    def product_block(step):
+    def take_right(step):
         block = row ^ step
         if not (isinstance(step, int) and step == 0):
             right_copy(step).wait_recv()
         base = pl.multiple_of(block * pairs, pairs)
         right32[pl.ds(base, pairs), :] = right_all[block].astype(F32)
+
+    def product_block(half, step):
+        block = row ^ step
+        base = pl.multiple_of(block * pairs, pairs)
         acc = None
         for k in range(cols):
-            term = left32[:, k : k + 1, :] * right32[pl.ds(base + k, rows, stride=cols), :][None]
+            term = (
+                left32[half * span : (half + 1) * span, k : k + 1, :]
+                * right32[pl.ds(base + k, rows, stride=cols), :][None]
+            )
             acc = term if acc is None else acc + term
-        part_send[block] = acc.reshape(pairs, hidden).astype(BF16)
+        part_send[block, half * part : (half + 1) * part, :] = acc.reshape(part, hidden).astype(
+            BF16
+        )
 
         @pl.when(block != col)
         def _():
-            part_copy(block, row, block, col ^ block).start()
-
-    product_block(0)
-    loop(1, side, product_block)
-
-    held = [part_send[col].astype(F32)]
-
+            part_copy(half, block, block, col ^ block).start()
+
+    take_right(0)
+    for half in range(HALVES):
+        product_block(half, 0)
     if side <= 4:
-        product = part_send[col].astype(F32)
-        for step in range(1, side):
-            part_copy(0, row, col ^ step, step).wait_recv()
-            product = product + part_recv[col ^ step].astype(F32)
+        for step in range(1, side // 2):
+            take_right(step)
+            for half in range(HALVES):
+                product_block(half, step)
+        for step in range(side // 2, side):
+            take_right(step)
+            product_block(0, step)
+        for half in range(1, HALVES):
+            for step in range(side // 2, side):
+                product_block(half, step)
     else:
 
-        def add_part(step, running):
-            part_copy(0, row, col ^ step, step).wait_recv()
-            return running + part_recv[col ^ step].astype(F32)
-
-        product = lax.fori_loop(1, side, add_part, held[0])
-
-    ohat, oinv = normalize(product)
-    mid = (ohat * mgain_ref[...] + mbias_ref[...]).astype(BF16)
-    value = dot(mid, po_ref[...])
+        def take_and_multiply(step):
+            take_right(step)
+            for half in range(HALVES):
+                product_block(half, step)
+
+        loop(1, side, take_and_multiply)
+
+    def grad_copy(half, step):
+        place = pl.ds(half * part, part)
+        return pltpu.make_async_remote_copy(
+            src_ref=grad_all.at[col, place],
+            dst_ref=grad_all.at[col, place],
+            send_sem=grad_ssem.at[half, step],
+            recv_sem=grad_rsem.at[half, step],
+            device_id=device(row, col ^ step),
+            device_id_type=MESH,
+        )
+
     upstream = cot_ref[...].reshape(pairs, chans).astype(F32)
     grad_value = (upstream * gate).astype(BF16)
-    grad_mid = dot_transposed(grad_value, po_ref[...])
-    grad_product = normalize_backward(grad_mid * mgain_ref[...], ohat, oinv)
-    grad_all[col] = grad_product.astype(BF16)
-
-    def grad_copy(step):
-        return pltpu.make_async_remote_copy(
-            src_ref=grad_all.at[col],
-            dst_ref=grad_all.at[col],
-            send_sem=grad_ssem.at[step],
-            recv_sem=grad_rsem.at[step],
-            device_id=device(row, col ^ step),
-            device_id_type=MESH,
-        )
-
-    loop(1, side, lambda step: grad_copy(step).start())
-
+    grad_mid = dot_transposed(grad_value, po_ref[...]) * mgain_ref[...]
+    values = []
+
+    for half in range(HALVES):
+        own = slice(half * part, (half + 1) * part)
+
+        def add_part(step, running):
+            part_copy(half, 0, col ^ step, step).wait_recv()
+            return running + part_recv[col ^ step, own, :].astype(F32)
+
+        product = part_send[col, own, :].astype(F32)
+        if side <= 4:
+            for step in range(1, side):
+                product = add_part(step, product)
+        else:
+            product = lax.fori_loop(1, side, add_part, product)
+        ohat, oinv = normalize(product)
+        grad_product = normalize_backward(grad_mid[own], ohat, oinv)
+        grad_all[col, own, :] = grad_product.astype(BF16)
+        loop(1, side, lambda step: grad_copy(half, step).start())
+        mid = (ohat * mgain_ref[...] + mbias_ref[...]).astype(BF16)
+        values.append(dot(mid, po_ref[...]))
+
+    value = jnp.concatenate(values, axis=0)
     update_ref[...] = (gate * value).astype(BF16).reshape(rows, cols, chans)
+    update_store = pltpu.make_async_copy(update_ref, update_hbm, store_sem.at[0])
+    update_store.start()
     grad_gpre = (upstream * value * gate * (1.0 - gate)).astype(BF16)
 
     def q_copy(slot, r, sem):
@@ -226,27 +306,38 @@
 
     lg_sum[...] = jnp.zeros_like(lg_sum)
 
-    def grad_block(step):
+    def grad_block(half, step):
         block = col ^ step
+        own = slice(half * part, (half + 1) * part)
+        mine = slice(half * span, (half + 1) * span)
         if not (isinstance(step, int) and step == 0):
-            grad_copy(step).wait_recv()
-        grad32[...] = grad_all[block].astype(F32).reshape(rows, cols, hidden)
+            grad_copy(half, step).wait_recv()
+        grad32[...] = grad_all[block, own, :].astype(F32).reshape(span, cols, hidden)
         for j in range(cols):
-            term = jnp.sum(grad32[:, j : j + 1, :] * left32[...], axis=0)
-            q_send[block, j * cols : (j + 1) * cols, :] = term.astype(BF16)
-
-        @pl.when(block != row)
-        def _():
-            q_copy(block, block, row ^ block).start()
-
-        acc = lg_sum[...]
+            term = jnp.sum(grad32[:, j : j + 1, :] * left32[mine], axis=0)
+            where = slice(j * cols, (j + 1) * cols)
+            if half > 0:
+                term = term + q_sum[block, where, :]
+            if half < HALVES - 1:
+                q_sum[block, where, :] = term
+            else:
+                q_send[block, where, :] = term.astype(BF16)
+
+        if half == HALVES - 1:
+
+            @pl.when(block != row)
+            def _():
+                q_copy(block, block, row ^ block).start()
+
+        acc = lg_sum[mine]
         base = pl.multiple_of(block * pairs, pairs)
         for j in range(cols):
             acc = acc + grad32[:, j : j + 1, :] * right32[pl.ds(base + j * cols, cols), :][None]
-        lg_sum[...] = acc
-
-    grad_block(0)
-    loop(1, side, grad_block)
+        lg_sum[mine] = acc
+
+    for half in range(HALVES):
+        grad_block(half, 0)
+        loop(1, side, functools.partial(grad_block, half))
 
     def gating_back(grad_out, sig, val):
         masked = grad_out * pmask
@@ -295,19 +386,44 @@
     pgrad_ref[...] = normalize_backward(
         normalized_gradient * gain_ref[...], xhat, inverse
     ).reshape(rows, cols, chans)
+    pgrad_store = pltpu.make_async_copy(pgrad_ref, pgrad_hbm, store_sem.at[1])
+    pgrad_store.start()
 
     def sent(step):
         right_copy(step).wait_send()
-        part_copy(0, row, col ^ step, step).wait_send()
-        grad_copy(step).wait_send()
+        for half in range(HALVES):
+            part_copy(half, 0, col ^ step, step).wait_send()
+            grad_copy(half, step).wait_send()
         q_copy(0, row ^ step, step).wait_send()
 
     loop(1, side, sent)
     pltpu.make_async_copy(stat_recv, stat_recv, stat_rsem).wait()
     stats = stat_send[...] + jnp.sum(stat_recv[...], axis=0)
-    bgrad_ref[...] = stats[0:1, :] / total
-    ggrad_ref[...] = stats[1:2, :] / total
+    stats_ref[...] = stats / total
+    stats_store = pltpu.make_async_copy(stats_ref, stats_hbm, store_sem.at[2])
+    stats_store.start()
     pltpu.make_async_copy(stat_recv, stat_recv, stat_ssem).wait()
+    update_store.wait()
+    pgrad_store.wait()
+    stats_store.wait()
+
+
+def finish(update_ref, pgrad_ref, stats_ref, update_hbm, pgrad_hbm, ggrad_hbm, bgrad_hbm, sem):
+    copies = [
+        pltpu.make_async_copy(source, target, sem.at[index])
+        for index, (source, target) in enumerate(
+            (
+                (pgrad_ref, pgrad_hbm),
+                (update_ref, update_hbm),
+                (stats_ref.at[1:2], ggrad_hbm),
+                (stats_ref.at[0:1], bgrad_hbm),
+            )
+        )
+    ]
+    for copy in copies:
+        copy.start()
+    for copy in copies:
+        copy.wait()
 
 
 def on_device(
@@ -328,35 +444,54 @@
     hidden = proj_left.shape[1] // 2
     pairs = rows * cols
     blocks = (side, pairs, hidden)
-    vmem = pl.BlockSpec(memory_space=pltpu.VMEM)
-    update, pair_gradient, gain_gradient, grad_bias = pl.pallas_call(
+    hbm = pl.BlockSpec(memory_space=pltpu.HBM)
+    block = (rows, cols, chans)
+    update, pair_gradient, stats = pl.pallas_call(
         functools.partial(kernel, side),
         out_shape=(
             jax.ShapeDtypeStruct((rows, cols, chans), BF16),
             jax.ShapeDtypeStruct((rows, cols, chans), F32),
-            jax.ShapeDtypeStruct((1, chans), F32),
-            jax.ShapeDtypeStruct((1, chans), F32),
+            jax.ShapeDtypeStruct((2, chans), F32),
         ),
-        in_specs=[vmem] * 11,
-        out_specs=(vmem,) * 4,
+        in_specs=[hbm] * 11,
+        out_specs=(hbm,) * 3,
         scratch_shapes=[
+            pltpu.VMEM(block, BF16),
+            pltpu.VMEM(block, F32),
+            pltpu.VMEM((2, chans), F32),
+            pltpu.VMEM(block, BF16),
+            pltpu.VMEM((1, res_mask.shape[0]), jnp.int32),
+            pltpu.VMEM((1, chans), F32),
+            pltpu.VMEM((1, chans), F32),
+            pltpu.VMEM(proj_left.shape, BF16),
+            pltpu.VMEM(proj_right.shape, BF16),
+            pltpu.VMEM(gate_out.shape, BF16),
+            pltpu.VMEM((1, hidden), F32),
+            pltpu.VMEM((1, hidden), F32),
+            pltpu.VMEM(proj_out.shape, BF16),
+            pltpu.VMEM(block, BF16),
+            pltpu.SemaphoreType.DMA((11,)),
+            pltpu.SemaphoreType.DMA((3,)),
             pltpu.VMEM(blocks, BF16),
             pltpu.VMEM((side * pairs, hidden), F32),
             pltpu.VMEM((rows, cols, hidden), F32),
             pltpu.VMEM(blocks, BF16),
             pltpu.VMEM(blocks, BF16),
             pltpu.VMEM(blocks, BF16),
+            pltpu.VMEM((rows // HALVES, cols, hidden), F32),
             pltpu.VMEM((rows, cols, hidden), F32),
-            pltpu.VMEM((rows, cols, hidden), F32),
+            pltpu.VMEM(blocks, F32),
             pltpu.VMEM(blocks, BF16),
             pltpu.VMEM(blocks, BF16),
             pltpu.VMEM((2, chans), F32),
             pltpu.VMEM((side * side - 1, 2, chans), F32),
         ]
-        + [pltpu.SemaphoreType.DMA((side,))] * 8
+        + [pltpu.SemaphoreType.DMA((side,))] * 2
+        + [pltpu.SemaphoreType.DMA((HALVES, side))] * 4
+        + [pltpu.SemaphoreType.DMA((side,))] * 2
         + [pltpu.SemaphoreType.DMA] * 2,
         compiler_params=pltpu.CompilerParams(
-            collective_id=0, has_side_effects=True, vmem_limit_bytes=40 * 1024 * 1024
+            collective_id=0, has_side_effects=True, vmem_limit_bytes=VMEM_LIMIT
         ),
         name="triangle",
     )(
@@ -372,6 +507,20 @@
         proj_out,
         cotangent,
     )
+    update, pair_gradient, gain_gradient, grad_bias = pl.pallas_call(
+        finish,
+        out_shape=(
+            jax.ShapeDtypeStruct(block, BF16),
+            jax.ShapeDtypeStruct(block, F32),
+            jax.ShapeDtypeStruct((1, chans), F32),
+            jax.ShapeDtypeStruct((1, chans), F32),
+        ),
+        in_specs=[hbm] * 3,
+        out_specs=(hbm,) * 4,
+        scratch_shapes=[pltpu.SemaphoreType.DMA((4,))],
+        compiler_params=pltpu.CompilerParams(vmem_limit_bytes=VMEM_LIMIT),
+        name="finish",
+    )(update, pair_gradient, stats)
     return update, pair_gradient, gain_gradient.reshape(-1), grad_bias.reshape(-1)
 
 

time: 42.4 us -> 41 us (0.967)
  local copies, waits for them, and re-layouts: 7.86 us -> 0 us
  Pallas kernels: 33.4 us -> 40.2 us
    unnamed x26 -> x0, local copies, waits for them, and re-layouts: 7.86 us -> none
    pallas_call x0 -> x1, Pallas kernels: none -> 7.13 us  [on_device(): pl.pallas_call(finish, out_shape=(jax.ShapeDtypeStruct(block, BF16), jax....]
where the time goes in v2:
time: 41 us; the launch traced here: 40.8 us
  Pallas kernels  40.2 us (98%)
  between operations  0.64 us (2%)
    pallas_call x1, Pallas kernels, on_device(): pl.pallas_call(functools.partial(kernel, side), out_shape=(jax.ShapeDtype...  33 us
    pallas_call x1, Pallas kernels, on_device(): pl.pallas_call(finish, out_shape=(jax.ShapeDtypeStruct(block, BF16), jax....  7.13 us

profile of v2, /device:TPU:0, one launch (start us, length us, event | category | flops | bytes accessed | tf_op | source)
XLA Modules:
  0.0 40.8 jit_solution(4901582889066108281)
XLA Ops:
  0.6 33.0 %triangle.1 = (bf16[16,16,128]{2,1,0:T(8,128)(2,1)}, f32[16,16,128]{2,1,0:T(8,128)}, f32[2,128]{1,0:T(2,128)}) custom-call(bf16[16,16,128]{2,1,0:T(8,128)(2,1)} %pair_hbm.1, s32[1,64]{1,0:T(1,128)} %bitcast.7, f32[1,128]{1,0:T(1,128)} %bitcast.8, f32[1,128]{1,0:T(1,128)} %bitcast.9, bf16[128,256]{1,0:T(8,128)(2,1)} %pl_hbm.1, bf16[128,256]{1,0:T(8,128)(2,1)} %pr_hbm.1, ...), custom_call_target="tpu_custom_call" | custom-call | tf_op jit(solution)/shard_map/triangle/pallas_call | solution.py:449
  33.7 7.1 %finish.1 = (bf16[16,16,128]{2,1,0:T(8,128)(2,1)}, f32[16,16,128]{2,1,0:T(8,128)}, f32[1,128]{1,0:T(1,128)}, f32[1,128]{1,0:T(1,128)}) custom-call(bf16[16,16,128]{2,1,0:T(8,128)(2,1)} %get-tuple-element.11.update_ref, f32[16,16,128]{2,1,0:T(8,128)} %get-tuple-element.12.pgrad_ref, f32[2,128]{1,0:T(2,128)} %get-tuple-element.13.stats_ref), custom_call_target="tpu_custom_call" | custom-call | tf_op jit(solution)/shard_map/finish/pallas_call | solution.py:510

commit v3 on v2

--- a/solution.py
+++ b/solution.py
@@ -408,22 +408,34 @@
     stats_store.wait()
 
 
-def finish(update_ref, pgrad_ref, stats_ref, update_hbm, pgrad_hbm, ggrad_hbm, bgrad_hbm, sem):
-    copies = [
+def finish(
+    update_in, pgrad_in, stats_in, update_out, pgrad_out, ggrad_out, bgrad_out, update, pgrad, stats, sem
+):
+    loads = [
         pltpu.make_async_copy(source, target, sem.at[index])
         for index, (source, target) in enumerate(
+            ((pgrad_in, pgrad), (update_in, update), (stats_in, stats))
+        )
+    ]
+    stores = [
+        pltpu.make_async_copy(source, target, sem.at[index + 3])
+        for index, (source, target) in enumerate(
             (
-                (pgrad_ref, pgrad_hbm),
-                (update_ref, update_hbm),
-                (stats_ref.at[1:2], ggrad_hbm),
-                (stats_ref.at[0:1], bgrad_hbm),
+                (pgrad, pgrad_out),
+                (update, update_out),
+                (stats.at[1:2], ggrad_out),
+                (stats.at[0:1], bgrad_out),
             )
         )
     ]
-    for copy in copies:
-        copy.start()
-    for copy in copies:
-        copy.wait()
+    for load in loads:
+        load.start()
+    for index in (2, 1, 0):
+        loads[index].wait()
+        for store in stores[index : 4 if index == 2 else index + 1]:
+            store.start()
+    for store in stores:
+        store.wait()
 
 
 def on_device(
@@ -517,7 +529,12 @@
         ),
         in_specs=[hbm] * 3,
         out_specs=(hbm,) * 4,
-        scratch_shapes=[pltpu.SemaphoreType.DMA((4,))],
+        scratch_shapes=[
+            pltpu.VMEM(block, BF16),
+            pltpu.VMEM(block, F32),
+            pltpu.VMEM((2, chans), F32),
+            pltpu.SemaphoreType.DMA((7,)),
+        ],
         compiler_params=pltpu.CompilerParams(vmem_limit_bytes=VMEM_LIMIT),
         name="finish",
     )(update, pair_gradient, stats)

time: 41 us -> 35.5 us (0.87)
  Pallas kernels: 40.2 us -> 34.7 us
    pallas_call x1, Pallas kernels: 7.13 us -> 1.65 us  [on_device(): pl.pallas_call(finish, out_shape=(jax.ShapeDtypeStruct(block, BF16), jax....]
where the time goes in v3:
time: 35.5 us; the launch traced here: 35.3 us
  Pallas kernels  34.7 us (98%)
  between operations  0.64 us (2%)
    pallas_call x1, Pallas kernels, on_device(): pl.pallas_call(functools.partial(kernel, side), out_shape=(jax.ShapeDtype...  33 us
    pallas_call x1, Pallas kernels, on_device(): pl.pallas_call(finish, out_shape=(jax.ShapeDtypeStruct(block, BF16), jax....  1.65 us

profile of v3, /device:TPU:0, one launch (start us, length us, event | category | flops | bytes accessed | tf_op | source)
XLA Modules:
  0.0 35.3 jit_solution(1802301122220453681)
XLA Ops:
  0.6 33.0 %triangle.1 = (bf16[16,16,128]{2,1,0:T(8,128)(2,1)}, f32[16,16,128]{2,1,0:T(8,128)}, f32[2,128]{1,0:T(2,128)}) custom-call(bf16[16,16,128]{2,1,0:T(8,128)(2,1)} %pair_hbm.1, s32[1,64]{1,0:T(1,128)} %bitcast.7, f32[1,128]{1,0:T(1,128)} %bitcast.8, f32[1,128]{1,0:T(1,128)} %bitcast.9, bf16[128,256]{1,0:T(8,128)(2,1)} %pl_hbm.1, bf16[128,256]{1,0:T(8,128)(2,1)} %pr_hbm.1, ...), custom_call_target="tpu_custom_call" | custom-call | tf_op jit(solution)/shard_map/triangle/pallas_call | solution.py:461
  33.7 1.6 %finish.1 = (bf16[16,16,128]{2,1,0:T(8,128)(2,1)}, f32[16,16,128]{2,1,0:T(8,128)}, f32[1,128]{1,0:T(1,128)}, f32[1,128]{1,0:T(1,128)}) custom-call(bf16[16,16,128]{2,1,0:T(8,128)(2,1)} %get-tuple-element.11.update_in, f32[16,16,128]{2,1,0:T(8,128)} %get-tuple-element.12.pgrad_in, f32[2,128]{1,0:T(2,128)} %get-tuple-element.13.stats_in), custom_call_target="tpu_custom_call" | custom-call | tf_op jit(solution)/shard_map/finish/pallas_call | solution.py:522

commit v4 on v3

--- a/solution.py
+++ b/solution.py
@@ -179,7 +179,18 @@
             device_id_type=MESH,
         )
 
-    loop(1, side, lambda step: right_copy(step).start())
+    right_copy(1).start()
+    loop(1, side // 2, lambda half_step: right_copy(2 * half_step).start())
+
+    def right_relay(step):
+        return pltpu.make_async_remote_copy(
+            src_ref=right_all.at[row ^ step],
+            dst_ref=right_all.at[row ^ step],
+            send_sem=right_ssem.at[step + 1],
+            recv_sem=right_rsem.at[step + 1],
+            device_id=device(row ^ 1, col),
+            device_id_type=MESH,
+        )
 
     for load in loads[5:]:
         load.wait()
@@ -208,6 +219,15 @@
         block = row ^ step
         if not (isinstance(step, int) and step == 0):
             right_copy(step).wait_recv()
+            if isinstance(step, int):
+                if step % 2 == 0:
+                    right_relay(step).start()
+            else:
+
+                @pl.when(lax.rem(step, 2) == 0)
+                def _():
+                    right_relay(step).start()
+
         base = pl.multiple_of(block * pairs, pairs)
         right32[pl.ds(base, pairs), :] = right_all[block].astype(F32)
 
@@ -233,15 +253,9 @@
     for half in range(HALVES):
         product_block(half, 0)
     if side <= 4:
-        for step in range(1, side // 2):
+        for step in range(1, side):
             take_right(step)
             for half in range(HALVES):
-                product_block(half, step)
-        for step in range(side // 2, side):
-            take_right(step)
-            product_block(0, step)
-        for half in range(1, HALVES):
-            for step in range(side // 2, side):
                 product_block(half, step)
     else:
 
@@ -306,15 +320,17 @@
 
     lg_sum[...] = jnp.zeros_like(lg_sum)
 
-    def grad_block(half, step):
-        block = col ^ step
+    def take_grad(half, step):
         own = slice(half * part, (half + 1) * part)
-        mine = slice(half * span, (half + 1) * span)
         if not (isinstance(step, int) and step == 0):
             grad_copy(half, step).wait_recv()
-        grad32[...] = grad_all[block, own, :].astype(F32).reshape(span, cols, hidden)
+        grad32[col ^ step] = grad_all[col ^ step, own, :].astype(F32).reshape(span, cols, hidden)
+
+    def scatter_block(half, step):
+        block = col ^ step
+        mine = slice(half * span, (half + 1) * span)
         for j in range(cols):
-            term = jnp.sum(grad32[:, j : j + 1, :] * left32[mine], axis=0)
+            term = jnp.sum(grad32[block, :, j : j + 1, :] * left32[mine], axis=0)
             where = slice(j * cols, (j + 1) * cols)
             if half > 0:
                 term = term + q_sum[block, where, :]
@@ -329,15 +345,31 @@
             def _():
                 q_copy(block, block, row ^ block).start()
 
+    def gather_block(half, step):
+        block = col ^ step
+        mine = slice(half * span, (half + 1) * span)
         acc = lg_sum[mine]
         base = pl.multiple_of(block * pairs, pairs)
         for j in range(cols):
-            acc = acc + grad32[:, j : j + 1, :] * right32[pl.ds(base + j * cols, cols), :][None]
+            acc = (
+                acc
+                + grad32[block, :, j : j + 1, :]
+                * right32[pl.ds(base + j * cols, cols), :][None]
+            )
         lg_sum[mine] = acc
 
     for half in range(HALVES):
-        grad_block(half, 0)
-        loop(1, side, functools.partial(grad_block, half))
+
+        def scatter_step(step):
+            take_grad(half, step)
+            scatter_block(half, step)
+            if half < HALVES - 1:
+                gather_block(half, step)
+
+        scatter_step(0)
+        loop(1, side, scatter_step)
+    gather_block(HALVES - 1, 0)
+    loop(1, side, functools.partial(gather_block, HALVES - 1))
 
     def gating_back(grad_out, sig, val):
         masked = grad_out * pmask
@@ -490,7 +522,7 @@
             pltpu.VMEM(blocks, BF16),
             pltpu.VMEM(blocks, BF16),
             pltpu.VMEM(blocks, BF16),
-            pltpu.VMEM((rows // HALVES, cols, hidden), F32),
+            pltpu.VMEM((side, rows // HALVES, cols, hidden), F32),
             pltpu.VMEM((rows, cols, hidden), F32),
             pltpu.VMEM(blocks, F32),
             pltpu.VMEM(blocks, BF16),

time: 35.5 us -> 35 us (0.986)
  Pallas kernels: 34.7 us -> 34.1 us
    pallas_call x1, Pallas kernels: 33 us -> 32.5 us  [on_device(): pl.pallas_call(functools.partial(kernel, side), out_shape=(jax.ShapeDtype...]
where the time goes in v4:
time: 35 us; the launch traced here: 34.8 us
  Pallas kernels  34.1 us (97%)
  between operations  0.64 us (2%)
    pallas_call x1, Pallas kernels, on_device(): pl.pallas_call(functools.partial(kernel, side), out_shape=(jax.ShapeDtype...  32.5 us
    pallas_call x1, Pallas kernels, on_device(): pl.pallas_call(finish, out_shape=(jax.ShapeDtypeStruct(block, BF16), jax....  1.65 us

profile of v4, /device:TPU:0, one launch (start us, length us, event | category | flops | bytes accessed | tf_op | source)
XLA Modules:
  0.0 34.8 jit_solution(9031390245902651116)
XLA Ops:
  0.6 32.5 %triangle.1 = (bf16[16,16,128]{2,1,0:T(8,128)(2,1)}, f32[16,16,128]{2,1,0:T(8,128)}, f32[2,128]{1,0:T(2,128)}) custom-call(bf16[16,16,128]{2,1,0:T(8,128)(2,1)} %pair_hbm.1, s32[1,64]{1,0:T(1,128)} %bitcast.7, f32[1,128]{1,0:T(1,128)} %bitcast.8, f32[1,128]{1,0:T(1,128)} %bitcast.9, bf16[128,256]{1,0:T(8,128)(2,1)} %pl_hbm.1, bf16[128,256]{1,0:T(8,128)(2,1)} %pr_hbm.1, ...), custom_call_target="tpu_custom_call" | custom-call | tf_op jit(solution)/shard_map/triangle/pallas_call | solution.py:493
  33.1 1.6 %finish.1 = (bf16[16,16,128]{2,1,0:T(8,128)(2,1)}, f32[16,16,128]{2,1,0:T(8,128)}, f32[1,128]{1,0:T(1,128)}, f32[1,128]{1,0:T(1,128)}) custom-call(bf16[16,16,128]{2,1,0:T(8,128)(2,1)} %get-tuple-element.11.update_in, f32[16,16,128]{2,1,0:T(8,128)} %get-tuple-element.12.pgrad_in, f32[2,128]{1,0:T(2,128)} %get-tuple-element.13.stats_in), custom_call_target="tpu_custom_call" | custom-call | tf_op jit(solution)/shard_map/finish/pallas_call | solution.py:554
